TPU v7x, 32 devices: a whole 2x2x4 slice. The times are simulated.
32 devices in a mesh: section: 4 (over y, x), shard: 8 (over z, core).
Axes of the slice: x: 2, y: 2, z: 4, core: 2. Of those that a mesh axis runs over, the one named last changes fastest.
Arguments:
- memory: bfloat16 [8192, 512], P('shard'), may hold values from -6 to 6
- messages: bfloat16 [2, 8, 8, 4, 512], P(None, 'shard', None, 'section'), may hold values from -6 to 6
- slot_rows: int32 [2, 8, 8, 4], P(None, 'shard', None, 'section'), may hold values from 0 to 1023, as said below
- counts: int32 [2, 8, 8], P(None, 'shard'), may hold values from 0 to 4, as said below
- src_slot: int32 [2, 4096], P(None, ('section', 'shard')), may hold values from 0 to 7
- nbr_slots: int32 [2, 4096, 10], P(None, ('section', 'shard')), may hold values from 0 to 7
- time_gap: float32 [2, 4096, 10], P(None, ('section', 'shard')), may hold values from 0.1 to 100
- time_freq: float32 [128], replicated, may hold values from 0.01 to 1
- time_phase: float32 [128], replicated, may hold values from -3.140625 to 3.140625
- gru_input: bfloat16 [512, 1536], P('section'), may hold values from -0.25 to 0.25
- gru_hidden: bfloat16 [512, 1536], P('section'), may hold values from -0.25 to 0.25
- gru_bias: float32 [2, 1536], replicated, may hold values from -3 to 3
- attn_qkv: bfloat16 [512, 1536], P('section'), may hold values from -0.25 to 0.25
- attn_out: bfloat16 [512, 512], P('section'), may hold values from -0.25 to 0.25
- time_proj: bfloat16 [128, 1024], P('section'), may hold values from -0.5 to 0.5
Outputs:
- memory_out: bfloat16 [8192, 512], P('shard')
- embeddings: bfloat16 [2, 4096, 512], P(None, ('section', 'shard'))
Inputs may be any that keep to these rules, and one draw needn't show every extreme that they name: `slot_rows`: within one batch the rows of one owner named by all devices' slots are distinct. `counts`: in every batch one owner receives 4 live slots from every device.
All inputs are finite; a program needn't handle non-finite values.
Results may differ from a plain program's by a relative error of at most 0.015.
Values may be sent and summed in bfloat16 or wider, within the bound.
A program may use at most 128 MiB of HBM per device.

v0:
```python
import jax
import jax.numpy as jnp
from jax import lax
from jax.sharding import PartitionSpec as P

HEADS = 2
HD = 256
BATCHES = 2


def gru_rows(x, h, w_in, w_hid, bias):
    width = x.shape[1]
    gx = jnp.dot(x, w_in, preferred_element_type=jnp.float32) + bias[0]
    gh = jnp.dot(h, w_hid, preferred_element_type=jnp.float32) + bias[1]
    reset = jax.nn.sigmoid(gx[:, :width] + gh[:, :width])
    update = jax.nn.sigmoid(gx[:, width : 2 * width] + gh[:, width : 2 * width])
    fresh = jnp.tanh(gx[:, 2 * width :] + reset * gh[:, 2 * width :])
    return ((1.0 - update) * fresh + update * h.astype(jnp.float32)).astype(jnp.bfloat16)


def embed(pool, source, nearby, gaps, freq, phase, qkv, out_w, tproj):
    width = pool.shape[1]
    kv = jnp.dot(pool, qkv[:, width:], preferred_element_type=jnp.float32).astype(jnp.bfloat16)
    query = jnp.dot(pool[source], qkv[:, :width], preferred_element_type=jnp.float32)
    encoded = jnp.cos(gaps[..., None] * freq + phase).astype(jnp.bfloat16)
    timed = jnp.einsum("ent,tc->enc", encoded, tproj, preferred_element_type=jnp.float32)
    near = kv[nearby].astype(jnp.float32) + timed
    scale = 1.0 / jnp.sqrt(jnp.float32(HD))
    pieces = []
    for head in range(HEADS):
        low = head * HD
        keys = near[:, :, low : low + HD]
        values = near[:, :, width + low : width + low + HD]
        scores = jnp.einsum("ed,end->en", query[:, low : low + HD], keys) * scale
        weights = jax.nn.softmax(scores, axis=-1)
        pieces.append(jnp.einsum("en,end->ed", weights, values))
    mixed = jnp.concatenate(pieces, axis=1).astype(jnp.bfloat16)
    return jnp.dot(mixed, out_w, preferred_element_type=jnp.float32).astype(jnp.bfloat16)


def body(
    memory,
    messages,
    slot_rows,
    counts,
    src_slot,
    nbr_slots,
    time_gap,
    time_freq,
    time_phase,
    gru_input,
    gru_hidden,
    gru_bias,
    attn_qkv,
    attn_out,
    time_proj,
):
    rows_here = memory.shape[0]
    width = memory.shape[1]
    owners = slot_rows.shape[2]
    quarter = slot_rows.shape[3]
    section_pos = lax.axis_index("section")
    full_in, full_hid, full_qkv, full_out, full_proj = (
        lax.all_gather(gru_input, "section", axis=0, tiled=True),
        lax.all_gather(gru_hidden, "section", axis=0, tiled=True),
        lax.all_gather(attn_qkv, "section", axis=0, tiled=True),
        lax.all_gather(attn_out, "section", axis=0, tiled=True),
        lax.all_gather(time_proj, "section", axis=0, tiled=True),
    )
    outputs = []
    for batch in range(BATCHES):
        wanted = slot_rows[batch, 0]
        places = section_pos * quarter + jnp.arange(quarter, dtype=jnp.int32)
        alive = (places[None, :] < counts[batch, 0][:, None]).astype(jnp.int32)
        got_rows, got_alive = (
            lax.all_to_all(wanted, "shard", split_axis=0, concat_axis=0, tiled=True),
            lax.all_to_all(alive, "shard", split_axis=0, concat_axis=0, tiled=True),
        )
        picked = jnp.where(got_alive[..., None] == 1, memory[got_rows], jnp.zeros((), jnp.bfloat16))
        fetched = lax.all_to_all(picked, "shard", split_axis=0, concat_axis=0, tiled=True)
        updated = gru_rows(
            messages[batch, 0].reshape(owners * quarter, width),
            fetched.reshape(owners * quarter, width),
            full_in,
            full_hid,
            gru_bias,
        )
        returned = lax.all_to_all(
            updated.reshape(owners, quarter, width),
            "shard",
            split_axis=0,
            concat_axis=0,
            tiled=True,
        )
        new_rows, new_places, new_alive = (
            lax.all_gather(returned, "section", axis=1, tiled=True),
            lax.all_gather(got_rows, "section", axis=1, tiled=True),
            lax.all_gather(got_alive, "section", axis=1, tiled=True),
        )
        target = jnp.where(new_alive == 1, new_places, rows_here).reshape(-1)
        memory = memory.at[target].set(new_rows.reshape(-1, width), mode="drop")
        outputs.append(
            embed(
                updated,
                src_slot[batch],
                nbr_slots[batch],
                time_gap[batch],
                time_freq,
                time_phase,
                full_qkv,
                full_out,
                full_proj,
            )
        )
    return (memory, jnp.stack(outputs))


def solution(mesh):
    in_specs = (
        P("shard", None),
        P(None, "shard", None, "section", None),
        P(None, "shard", None, "section"),
        P(None, "shard", None),
        P(None, ("section", "shard")),
        P(None, ("section", "shard"), None),
        P(None, ("section", "shard"), None),
        P(),
        P(),
        P("section", None),
        P("section", None),
        P(),
        P("section", None),
        P("section", None),
        P("section", None),
    )
    out_specs = (P("shard", None), P(None, ("section", "shard"), None))
    return jax.shard_map(body, mesh=mesh, in_specs=in_specs, out_specs=out_specs, check_vma=False)
```

profile of v0, /device:TPU:0, one launch (start us, length us, event | category | flops | bytes accessed | tf_op | source)
XLA Modules:
  0.0 216.1 jit_solution(570774555276366415)
XLA Ops:
  7.3 1.3 copy.182
  8.6 0.7 all-gather.8.cloned.1.call-update
  9.4 0.7 copy.79
  10.0 6.3 %all-to-all-start.1 = ((s32[8,1,1]{2,1,0:T(1,128)}), s32[8,1,1]{2,1,0:T(1,128)S(1)}, u32[]{:S(2)}, u32[]{:S(2)}) async-start(s32[8,1,1]{2,1,0:T(1,128)} %copy.79), calls=%async_computation.1 | async-start | bytes 8192 | tf_op jit(solution)/shard_map/all_to_all | solution.py:76
  16.4 0.7 all-gather.12.cloned.1.call-update
  17.1 0.7 copy.77
  17.8 13.7 %all_gather.43 = bf16[512,512]{1,0:T(8,128)(2,1)} all-gather(bf16[128,512]{1,0:T(8,128)(2,1)S(1)} %copy-done.5), channel_id=1, replica_groups=mesh['section'=4,'shard'=8] {'section'}, dimensions={0}, use_global_device_ids=true | all-gather | bytes 655360 | tf_op jit(solution)/shard_map/all_gather | solution.py:67
  31.9 10.8 %all_gather.42 = bf16[128,1024]{1,0:T(8,128)(2,1)S(1)} all-gather(bf16[32,1024]{1,0:T(8,128)(2,1)S(1)} %copy-done.6), channel_id=1, replica_groups=mesh['section'=4,'shard'=8] {'section'}, dimensions={0}, use_global_device_ids=true | all-gather | bytes 327680 | tf_op jit(solution)/shard_map/all_gather | solution.py:68
  42.7 0.6 pad_clamp_fusion.2
  43.6 0.6 copy_bitcast_fusion
  44.2 0.7 copy.88
  44.8 4.8 %all-to-all-start = ((s32[8,1,1]{2,1,0:T(1,128)}), s32[8,1,1]{2,1,0:T(1,128)S(1)}, u32[]{:S(2)}, u32[]{:S(2)}) async-start(s32[8,1,1]{2,1,0:T(1,128)} %copy.77), calls=%async_computation | async-start | bytes 8192 | tf_op jit(solution)/shard_map/all_to_all | solution.py:77
  49.8 5.5 %all-to-all-done = s32[8,1,1]{2,1,0:T(1,128)S(1)} async-done(((s32[8,1,1]{2,1,0:T(1,128)}), s32[8,1,1]{2,1,0:T(1,128)S(1)}, u32[]{:S(2)}, u32[]{:S(2)}) %all-to-all-start) | async-done | bytes 64 | tf_op jit(solution)/shard_map/all_to_all | solution.py:77
  55.2 3.3 %all-to-all-start.5 = ((s32[8,1,1]{2,1,0:T(1,128)}), s32[8,1,1]{2,1,0:T(1,128)S(1)}, u32[]{:S(2)}, u32[]{:S(2)}) async-start(s32[8,1,1]{2,1,0:T(1,128)} %copy.88), calls=%async_computation.5 | async-start | bytes 8192 | tf_op jit(solution)/shard_map/all_to_all | solution.py:76
  58.7 0.7 copy.86
  59.3 6.7 %all-gather.1 = s32[8,4,1]{0,2,1:T(1,128)S(1)} all-gather(s32[8,1,1]{0,2,1:T(1,128)S(1)} %copy.80), channel_id=3, replica_groups=mesh['section'=4,'shard'=8] {'section'}, dimensions={1}, use_global_device_ids=true | all-gather | bytes 160 | tf_op jit(solution)/shard_map/all_gather | solution.py:97
  66.1 8.1 %all-gather = s32[8,4,1]{0,2,1:T(1,128)S(1)} all-gather(s32[8,1,1]{0,2,1:T(1,128)S(1)} %copy.78), channel_id=2, replica_groups=mesh['section'=4,'shard'=8] {'section'}, dimensions={1}, use_global_device_ids=true | all-gather | bytes 160 | tf_op jit(solution)/shard_map/all_gather | solution.py:98
  74.6 0.6 gather_fusion
  76.0 0.5 reduce.12
  76.5 0.6 reshape.480
  77.1 5.0 %all-to-all-start.4 = ((s32[8,1,1]{2,1,0:T(1,128)}), s32[8,1,1]{2,1,0:T(1,128)S(1)}, u32[]{:S(2)}, u32[]{:S(2)}) async-start(s32[8,1,1]{2,1,0:T(1,128)} %copy.86), calls=%async_computation.4 | async-start | bytes 8192 | tf_op jit(solution)/shard_map/all_to_all | solution.py:77
  82.2 5.5 %all-to-all-done.4 = s32[8,1,1]{2,1,0:T(1,128)S(1)} async-done(((s32[8,1,1]{2,1,0:T(1,128)}), s32[8,1,1]{2,1,0:T(1,128)S(1)}, u32[]{:S(2)}, u32[]{:S(2)}) %all-to-all-start.4) | async-done | bytes 64 | tf_op jit(solution)/shard_map/all_to_all | solution.py:77
  87.8 3.3 %all-to-all-start.2 = ((bf16[8,2,256]{2,1,0:T(2,128)(2,1)}), bf16[8,2,256]{2,1,0:T(2,128)(2,1)S(1)}, u32[]{:S(2)}, u32[]{:S(2)}) async-start(bf16[8,2,256]{2,1,0:T(2,128)(2,1)} %reshape.480), calls=%async_computation.2 | async-start | bytes 16384 | tf_op jit(solution)/shard_map/all_to_all | solution.py:80
  91.1 6.8 %all-gather.3 = s32[8,4,1]{0,2,1:T(1,128)S(1)} all-gather(s32[8,1,1]{0,2,1:T(1,128)S(1)} %copy.89), channel_id=5, replica_groups=mesh['section'=4,'shard'=8] {'section'}, dimensions={1}, use_global_device_ids=true | all-gather | bytes 160 | tf_op jit(solution)/shard_map/all_gather | solution.py:97
  97.9 8.1 %all-gather.2 = s32[8,4,1]{0,2,1:T(1,128)S(1)} all-gather(s32[8,1,1]{0,2,1:T(1,128)S(1)} %copy.87), channel_id=4, replica_groups=mesh['section'=4,'shard'=8] {'section'}, dimensions={1}, use_global_device_ids=true | all-gather | bytes 160 | tf_op jit(solution)/shard_map/all_gather | solution.py:98
  106.7 0.6 fusion.88
  107.3 0.5 fusion.89
  107.9 1.7 convolution_add_fusion.2
  109.6 1.7 convolution_add_fusion.3
  111.4 0.6 reduce.13
  111.9 0.6 reshape.482
  112.5 5.0 %all-to-all-start.3 = ((bf16[8,2,256]{2,1,0:T(2,128)(2,1)}), bf16[8,2,256]{2,1,0:T(2,128)(2,1)S(1)}, u32[]{:S(2)}, u32[]{:S(2)}) async-start(bf16[8,2,256]{2,1,0:T(2,128)(2,1)} %reshape.482), calls=%async_computation.3 | async-start | bytes 16384 | tf_op jit(solution)/shard_map/all_to_all | solution.py:88
  117.5 1.5 convolution_convert_fusion.3
  119.0 4.3 %gather_fusion.3 = bf16[1280,1024]{1,0:T(8,128)(2,1)S(1)} fusion(bf16[8,1024]{1,0:T(8,128)(2,1)S(1)} %convolution_convert_fusion.3, s32[2048]{0:T(1024)S(1)} %pad_clamp_fusion.1), kind=kCustom, calls=%fused_computation.3 | custom fusion | bytes 5248000 | tf_op jit(solution)/shard_map/gather | solution.py:27
  123.3 3.7 %reshape.453 = f32[128,10,1024]{2,1,0:T(8,128)} reshape(bf16[1280,1024]{1,0:T(8,128)(2,1)S(1)} %gather_fusion.3) | data formatting | bytes 7864320 | tf_op jit(solution)/shard_map/convert_element_type | solution.py:27
  127.0 8.5 %copy_add_fusion.1 = bf16[128,10,1024]{2,0,1:T(8,128)(2,1)S(1)} fusion(f32[128,10,1024]{2,1,0:T(8,128)} %reshape.453, f32[128]{0:T(128)S(1)} %copy-done.12, f32[128]{0:T(128)S(1)} %copy-done.14, f32[128,10]{0,1:T(8,128)S(1)} %get-tuple-element.27, bf16[128,1024]{1,0:T(8,128)(2,1)S(1)} %all_gather.42), kind=kOutput, calls=%fused_computation.9 | convolution fusion | flops 338657280 | bytes 8132608 | tf_op jit(solution)/shard_map/ent,tc->enc/dot_general | solution.py:26
  135.5 1.2 fusion.94
  136.8 0.8 gather_fusion.2
  137.6 1.3 fusion.22
  138.9 1.7 fusion.10
  141.8 0.5 fusion.8
  142.3 0.9 convolution_add_fusion.1
  143.2 1.6 fusion.12
  144.9 7.0 %all_gather.37 = bf16[8,4,512]{2,0,1:T(8,128)(2,1)S(1)} all-gather(bf16[8,1,512]{2,0,1:T(8,128)(2,1)S(1)} %copy.84), channel_id=1, replica_groups=mesh['section'=4,'shard'=8] {'section'}, dimensions={1}, use_global_device_ids=true | all-gather | bytes 40960 | tf_op jit(solution)/shard_map/all_gather | solution.py:96
  151.9 3.1 %scatter_fusion = bf16[1024,512]{1,0:T(8,128)(2,1)} fusion(bf16[1024,512]{1,0:T(8,128)(2,1)} %copy-done.3, s32[32]{0:T(128)S(1)} %copy-done.20, bf16[32,512]{1,0:T(8,128)(2,1)S(1)} %reshape.427), kind=kCustom, calls=%fused_computation.6 | custom fusion | bytes 98432 | tf_op jit(solution)/shard_map/scatter | solution.py:101
  155.0 1.9 gather_fusion.1
  157.0 0.5 reduce.14
  157.6 0.6 reshape.484
  158.2 5.1 %all-to-all-start.6 = ((bf16[8,2,256]{2,1,0:T(2,128)(2,1)}), bf16[8,2,256]{2,1,0:T(2,128)(2,1)S(1)}, u32[]{:S(2)}, u32[]{:S(2)}) async-start(bf16[8,2,256]{2,1,0:T(2,128)(2,1)} %reshape.484), calls=%async_computation.6 | async-start | bytes 16384 | tf_op jit(solution)/shard_map/all_to_all | solution.py:80
  163.3 1.3 fusion.16
  164.5 4.3 %all-to-all-done.6 = bf16[8,2,256]{2,1,0:T(2,128)(2,1)S(1)} async-done(((bf16[8,2,256]{2,1,0:T(2,128)(2,1)}), bf16[8,2,256]{2,1,0:T(2,128)(2,1)S(1)}, u32[]{:S(2)}, u32[]{:S(2)}) %all-to-all-start.6) | async-done | bytes 8224 | tf_op jit(solution)/shard_map/all_to_all | solution.py:80
  169.3 0.6 reduce.15
  169.8 0.6 reshape.486
  170.4 3.3 %all-to-all-start.7 = ((bf16[8,2,256]{2,1,0:T(2,128)(2,1)}), bf16[8,2,256]{2,1,0:T(2,128)(2,1)S(1)}, u32[]{:S(2)}, u32[]{:S(2)}) async-start(bf16[8,2,256]{2,1,0:T(2,128)(2,1)} %reshape.486), calls=%async_computation.7 | async-start | bytes 16384 | tf_op jit(solution)/shard_map/all_to_all | solution.py:88
  173.7 1.5 convolution_convert_fusion.2
  175.2 4.3 %gather_fusion.5 = bf16[1280,1024]{1,0:T(8,128)(2,1)S(1)} fusion(bf16[8,1024]{1,0:T(8,128)(2,1)S(1)} %convolution_convert_fusion.2, s32[2048]{0:T(1024)S(1)} %pad_clamp_fusion), kind=kCustom, calls=%fused_computation.5 | custom fusion | bytes 5248000 | tf_op jit(solution)/shard_map/gather | solution.py:27
  179.5 3.7 %reshape.454 = f32[128,10,1024]{2,1,0:T(8,128)} reshape(bf16[1280,1024]{1,0:T(8,128)(2,1)S(1)} %gather_fusion.5) | data formatting | bytes 7864320 | tf_op jit(solution)/shard_map/convert_element_type | solution.py:27
  183.2 8.5 %copy_add_fusion = bf16[128,10,1024]{2,0,1:T(8,128)(2,1)S(1)} fusion(f32[128,10,1024]{2,1,0:T(8,128)} %reshape.454, f32[128,10]{0,1:T(8,128)S(1)} %copy-done.7, f32[128]{0:T(128)S(1)} %copy-done.13, f32[128]{0:T(128)S(1)} %copy-done.15, bf16[128,1024]{1,0:T(8,128)(2,1)S(1)} %all_gather.42), kind=kOutput, calls=%fused_computation.8 | convolution fusion | flops 338657280 | bytes 8132608 | tf_op jit(solution)/shard_map/ent,tc->enc/dot_general | solution.py:26
  192.1 1.0 gather_fusion.4
  193.1 1.3 fusion.20
  196.5 0.5 fusion.4
  197.3 0.7 pad_maximum_fusion
  198.0 8.4 %all_gather.40 = bf16[8,4,512]{2,0,1:T(8,128)(2,1)S(1)} all-gather(bf16[8,1,512]{2,0,1:T(8,128)(2,1)S(1)} %copy.93), channel_id=1, replica_groups=mesh['section'=4,'shard'=8] {'section'}, dimensions={1}, use_global_device_ids=true | all-gather | bytes 40960 | tf_op jit(solution)/shard_map/all_gather | solution.py:96
  206.5 3.1 %scatter_fusion.1 = bf16[1024,512]{1,0:T(8,128)(2,1)} fusion(bf16[1024,512]{1,0:T(8,128)(2,1)} %scatter_fusion, s32[32]{0:T(128)S(1)} %copy-done.19, bf16[32,512]{1,0:T(8,128)(2,1)S(1)} %reshape.435), kind=kCustom, calls=%fused_computation.7 | custom fusion | bytes 98432 | tf_op jit(solution)/shard_map/scatter | solution.py:101
  (131 shorter events, 7.4 us)
Async XLA Ops:
  7.2 2.2 %copy-start.16 = (s32[2,1,8,1]{2,3,1,0:T(1,128)S(1)}, s32[2,1,8,1]{2,3,1,0:T(1,128)}, u32[]{:S(2)}) copy-start(s32[2,1,8,1]{2,3,1,0:T(1,128)} %param.17) | copy-start | bytes 196
  7.2 9.9 %copy-start.17 = (s32[2,1,8]{2,1,0:T(1,128)S(1)}, s32[2,1,8]{2,1,0:T(1,128)}, u32[]{:S(2)}) copy-start(s32[2,1,8]{2,1,0:T(1,128)} %param.18) | copy-start | bytes 196
  7.2 35.5 %copy-start.18 = (s32[2,128]{1,0:T(2,128)S(1)}, s32[2,128]{1,0:T(2,128)}, u32[]{:S(2)}) copy-start(s32[2,128]{1,0:T(2,128)} %param.19) | copy-start | bytes 3076
  7.2 24.4 %copy-start.10 = (s32[2,128,10]{1,0,2:T(2,128)S(1)}, s32[2,128,10]{1,0,2:T(2,128)}, u32[]{:S(2)}) copy-start(s32[2,128,10]{1,0,2:T(2,128)} %param.20) | copy-start | bytes 30724
  7.2 24.6 %copy-start.11 = (f32[2,128,10]{1,0,2:T(2,128)S(1)}, f32[2,128,10]{1,0,2:T(2,128)}, u32[]{:S(2)}) copy-start(f32[2,128,10]{1,0,2:T(2,128)} %param.21) | copy-start | bytes 30724
  7.2 10.6 %copy-start.9 = (f32[2,1536]{1,0:T(2,128)S(1)}, f32[2,1536]{1,0:T(2,128)}, u32[]{:S(2)}) copy-start(f32[2,1536]{1,0:T(2,128)} %param.26) | copy-start | bytes 36868
  7.2 10.6 %copy-start.5 = (bf16[128,512]{1,0:T(8,128)(2,1)S(1)}, bf16[128,512]{1,0:T(8,128)(2,1)}, u32[]{:S(2)}) copy-start(bf16[128,512]{1,0:T(8,128)(2,1)} %param.28) | copy-start | bytes 393220
  7.2 24.6 %copy-start.6 = (bf16[32,1024]{1,0:T(8,128)(2,1)S(1)}, bf16[32,1024]{1,0:T(8,128)(2,1)}, u32[]{:S(2)}) copy-start(bf16[32,1024]{1,0:T(8,128)(2,1)} %param.29) | copy-start | bytes 196612
  7.2 100.6 %all-gather.10.cloned.1.call-start = ((), (), s32[]{:S(2)}) async-start(), calls=%async_computation.9 | async-start | bytes 1966080 | tf_op jit(solution)/shard_map/all_gather | solution.py:65
  8.6 101.0 %copy-start.3 = (bf16[1024,512]{1,0:T(8,128)(2,1)}, bf16[1024,512]{1,0:T(8,128)(2,1)S(1)}, u32[]{:S(2)}) copy-start(bf16[1024,512]{1,0:T(8,128)(2,1)S(1)} %copy.182) | copy-start | bytes 3145732
  8.6 101.0 %copy-start.8 = (bf16[2,1,8,1,512]{4,2,3,1,0:T(8,128)(2,1)S(1)}, bf16[2,1,8,1,512]{4,2,3,1,0:T(8,128)(2,1)}, u32[]{:S(2)}) copy-start(bf16[2,1,8,1,512]{4,2,3,1,0:T(8,128)(2,1)} %param.16) | copy-start | bytes 49156
  8.6 101.0 %all-gather.8.cloned.1.call-start = ((), (), s32[]{:S(2)}) async-start(), calls=%async_computation.8 | async-start | bytes 1966080 | tf_op jit(solution)/shard_map/all_gather | solution.py:64
  10.0 34.8 %all-to-all-start.1 = ((s32[8,1,1]{2,1,0:T(1,128)}), s32[8,1,1]{2,1,0:T(1,128)S(1)}, u32[]{:S(2)}, u32[]{:S(2)}) async-start(s32[8,1,1]{2,1,0:T(1,128)} %copy.79), calls=%async_computation.1 | async-start | bytes 8192 | tf_op jit(solution)/shard_map/all_to_all | solution.py:76
  16.4 101.2 %all-gather.12.cloned.1.call-start = ((), (), s32[]{:S(2)}) async-start(), calls=%async_computation.10 | async-start | bytes 1966080 | tf_op jit(solution)/shard_map/all_gather | solution.py:66
  44.8 10.4 %all-to-all-start = ((s32[8,1,1]{2,1,0:T(1,128)}), s32[8,1,1]{2,1,0:T(1,128)S(1)}, u32[]{:S(2)}, u32[]{:S(2)}) async-start(s32[8,1,1]{2,1,0:T(1,128)} %copy.77), calls=%async_computation | async-start | bytes 8192 | tf_op jit(solution)/shard_map/all_to_all | solution.py:77
  55.2 21.9 %all-to-all-start.5 = ((s32[8,1,1]{2,1,0:T(1,128)}), s32[8,1,1]{2,1,0:T(1,128)S(1)}, u32[]{:S(2)}, u32[]{:S(2)}) async-start(s32[8,1,1]{2,1,0:T(1,128)} %copy.88), calls=%async_computation.5 | async-start | bytes 8192 | tf_op jit(solution)/shard_map/all_to_all | solution.py:76
  77.1 10.6 %all-to-all-start.4 = ((s32[8,1,1]{2,1,0:T(1,128)}), s32[8,1,1]{2,1,0:T(1,128)S(1)}, u32[]{:S(2)}, u32[]{:S(2)}) async-start(s32[8,1,1]{2,1,0:T(1,128)} %copy.86), calls=%async_computation.4 | async-start | bytes 8192 | tf_op jit(solution)/shard_map/all_to_all | solution.py:77
  87.8 20.0 %all-to-all-start.2 = ((bf16[8,2,256]{2,1,0:T(2,128)(2,1)}), bf16[8,2,256]{2,1,0:T(2,128)(2,1)S(1)}, u32[]{:S(2)}, u32[]{:S(2)}) async-start(bf16[8,2,256]{2,1,0:T(2,128)(2,1)} %reshape.480), calls=%async_computation.2 | async-start | bytes 16384 | tf_op jit(solution)/shard_map/all_to_all | solution.py:80
  112.5 32.3 %all-to-all-start.3 = ((bf16[8,2,256]{2,1,0:T(2,128)(2,1)}), bf16[8,2,256]{2,1,0:T(2,128)(2,1)S(1)}, u32[]{:S(2)}, u32[]{:S(2)}) async-start(bf16[8,2,256]{2,1,0:T(2,128)(2,1)} %reshape.482), calls=%async_computation.3 | async-start | bytes 16384 | tf_op jit(solution)/shard_map/all_to_all | solution.py:88
  123.3 3.7 %copy-start.12 = (f32[128]{0:T(128)S(1)}, f32[128]{0:T(128)}, u32[]{:S(2)}) copy-start(f32[128]{0:T(128)} %param.23) | copy-start | bytes 1540
  123.3 3.7 %copy-start.14 = (f32[128]{0:T(128)S(1)}, f32[128]{0:T(128)}, u32[]{:S(2)}) copy-start(f32[128]{0:T(128)} %param.22) | copy-start | bytes 1540
  138.9 3.3 %copy-start.1 = (bf16[512,1536]{1,0:T(8,128)(2,1)S(1)}, bf16[512,1536]{1,0:T(8,128)(2,1)}, u32[]{:S(2)}) copy-start(bf16[512,1536]{1,0:T(8,128)(2,1)} %all-gather.8.cloned.1.call-done) | copy-start | bytes 4718596
  141.5 10.5 %copy-start.20 = (s32[32]{0:T(128)S(1)}, s32[32]{0:T(128)}, u32[]{:S(2)}) copy-start(s32[32]{0:T(128)} %fusion.88) | copy-start | bytes 388
  142.3 26.6 %copy-start = (bf16[512,1536]{1,0:T(8,128)(2,1)S(1)}, bf16[512,1536]{1,0:T(8,128)(2,1)}, u32[]{:S(2)}) copy-start(bf16[512,1536]{1,0:T(8,128)(2,1)} %all-gather.10.cloned.1.call-done) | copy-start | bytes 4718596
  143.2 26.0 %copy-start.4 = (f32[8,1536]{1,0:T(8,128)S(1)}, f32[8,1536]{1,0:T(8,128)}, u32[]{:S(2)}) copy-start(f32[8,1536]{1,0:T(8,128)} %convolution_add_fusion.1) | copy-start | bytes 147460
  158.2 10.7 %all-to-all-start.6 = ((bf16[8,2,256]{2,1,0:T(2,128)(2,1)}), bf16[8,2,256]{2,1,0:T(2,128)(2,1)S(1)}, u32[]{:S(2)}, u32[]{:S(2)}) async-start(bf16[8,2,256]{2,1,0:T(2,128)(2,1)} %reshape.484), calls=%async_computation.6 | async-start | bytes 16384 | tf_op jit(solution)/shard_map/all_to_all | solution.py:80
  170.4 27.6 %all-to-all-start.7 = ((bf16[8,2,256]{2,1,0:T(2,128)(2,1)}), bf16[8,2,256]{2,1,0:T(2,128)(2,1)S(1)}, u32[]{:S(2)}, u32[]{:S(2)}) async-start(bf16[8,2,256]{2,1,0:T(2,128)(2,1)} %reshape.486), calls=%async_computation.7 | async-start | bytes 16384 | tf_op jit(solution)/shard_map/all_to_all | solution.py:88
  179.5 3.7 %copy-start.7 = (f32[128,10]{0,1:T(8,128)S(1)}, f32[128,10]{0,1:T(8,128)}, u32[]{:S(2)}) copy-start(f32[128,10]{0,1:T(8,128)} %get-tuple-element.26) | copy-start | bytes 15364
  179.5 3.7 %copy-start.13 = (f32[128]{0:T(128)S(1)}, f32[128]{0:T(128)}, u32[]{:S(2)}) copy-start(f32[128]{0:T(128)} %param.23) | copy-start | bytes 1540
  179.5 3.7 %copy-start.15 = (f32[128]{0:T(128)S(1)}, f32[128]{0:T(128)}, u32[]{:S(2)}) copy-start(f32[128]{0:T(128)} %param.22) | copy-start | bytes 1540
  195.0 2.0 copy-start.2
  195.7 10.8 %copy-start.19 = (s32[32]{0:T(128)S(1)}, s32[32]{0:T(128)}, u32[]{:S(2)}) copy-start(s32[32]{0:T(128)} %fusion.89) | copy-start | bytes 388
Sparse Core Ops, SparseCore 0:
  9.9 37.3 all-gather.9
  49.1 30.9 all-gather.7
  82.0 30.9 all-gather.11
where the time goes:
time: 217 us; the launch traced here: 216 us
  blocking collectives  69.6 us (32%)
  local copies, waits for them, and re-layouts  37.8 us (17%)
  starting transfers between devices  36.3 us (17%)
  matrix products  35.1 us (16%)
  waiting for transfers between devices  16.7 us (8%)
  between operations  14.4 us (7%)
  other arithmetic  6.2 us (3%)
    dot_general x2, matrix products, embed(): jnp.einsum('ent,tc->enc', encoded, tproj, preferred_element_type=jnp.floa...  17.1 us
    all_gather x2, blocking collectives, body(): lax.all_gather(got_alive, 'section', axis=1, tiled=True)  16.2 us
    all_gather x2, blocking collectives, body(): lax.all_gather(returned, 'section', axis=1, tiled=True)  15.4 us
    all_gather x1, blocking collectives, body(): lax.all_gather(attn_out, 'section', axis=0, tiled=True)  13.7 us
    all_gather x2, blocking collectives, body(): lax.all_gather(got_rows, 'section', axis=1, tiled=True)  13.5 us
    all_to_all x2, waiting for transfers between devices, body(): lax.all_to_all(alive, 'shard', split_axis=0, concat_axis=0, tiled=True)  11 us
    all_gather x1, blocking collectives, body(): lax.all_gather(time_proj, 'section', axis=0, tiled=True)  10.8 us
    all_to_all x2, starting transfers between devices, body(): lax.all_to_all(alive, 'shard', split_axis=0, concat_axis=0, tiled=True)  9.87 us
  transfers between devices with their start and end apart: 11, of which 3 were waited for; matrix products, arithmetic and copies ran while one was open for 31% of the time, Pallas kernels for 0%

commit v1 on v0

v1 whole, which is shorter than its diff:
```python
import functools

import jax
import jax.numpy as jnp
from jax import lax
from jax.experimental import pallas as pl
from jax.experimental.pallas import tpu as pltpu
from jax.sharding import PartitionSpec as P

HEADS = 2
HD = 256
BATCHES = 2
MESH = pl.DeviceIdType.MESH
F32 = jnp.float32
BF16 = jnp.bfloat16
COS = (
    1.0,
    -0.5,
    0.0416666641831398,
    -0.0013888862449675798,
    2.480053444742225e-05,
    -2.753448029579886e-07,
    2.060102088918825e-09,
    -9.714491364110067e-12,
)


def cosine(x):
    turns = jnp.round(x * 0.15915494309189535)
    r = x - turns * 6.28125
    r = r - turns * 0.001935307179586232
    u = r * r
    total = jnp.full_like(u, COS[-1])
    for c in COS[-2::-1]:
        total = total * u + c
    return total


def dot(a, b, contract=(1, 0), precision=None):
    return lax.dot_general(
        a,
        b,
        (((contract[0],), (contract[1],)), ((), ())),
        preferred_element_type=F32,
        precision=precision,
    )


def split(x):
    high = x.astype(BF16)
    return high, (x - high.astype(F32)).astype(BF16)


def kernel(
    n_sec,
    n_shard,
    memory,
    messages,
    marks,
    src,
    nbr,
    gap,
    freq,
    phase,
    w_in,
    w_hid,
    bias,
    w_qkv,
    w_out,
    w_time,
    memory_out,
    emb,
    all_marks,
    x_src,
    x_all,
    picks_src0,
    picks_src1,
    picks0,
    picks1,
    part_src0,
    part_src1,
    part0,
    part1,
    back_src0,
    back_src1,
    back0,
    back1,
    hot0,
    hot1,
    gates_x,
    te,
    f_qkv,
    f_out,
    f_time,
    send_sems,
    recv_sems,
    bulk_send,
    bulk_recv,
    fwd_send,
    fwd_recv,
    own_sems,
):
    sec = lax.axis_index("section")
    shard = lax.axis_index("shard")
    devices = n_sec * n_shard
    me = sec * n_shard + shard
    nodes, width = memory.shape
    pool = n_shard
    cols = width // n_sec
    events = emb.shape[1]
    nbrs = gap.shape[1]
    tw = freq.shape[0]
    core = lax.rem(shard, 2)
    sibling = shard + 1 - 2 * core
    picks_src, picks = (picks_src0, picks_src1), (picks0, picks1)
    part_src, part = (part_src0, part_src1), (part0, part1)
    back_src, back = (back_src0, back_src1), (back0, back1)
    hot = (hot0, hot1)

    def drain(ref, sem):
        pltpu.make_async_copy(ref, ref, sem).wait()

    def to_all(step):
        def go(j, carry):
            peer = lax.rem(me + j, devices)
            step(lax.div(peer, n_shard), lax.rem(peer, n_shard))
            return carry

        lax.fori_loop(1, devices, go, 0)

    barrier = pltpu.get_barrier_semaphore()
    to_all(
        lambda s, d: pl.semaphore_signal(barrier, inc=1, device_id=(s, d), device_id_type=MESH)
    )

    for s in range(n_sec):
        x_src[s] = messages[:, s * cols : (s + 1) * cols].astype(F32)
    x_all[sec] = x_src[sec]
    all_marks[me] = marks[...]
    weights = ((w_qkv, f_qkv), (w_out, f_out), (w_time, f_time))
    own = []
    for i, (w, full) in enumerate(weights):
        k = w.shape[0]
        copy = pltpu.make_async_copy(
            w, full.at[pl.ds(pl.multiple_of(sec * k, k), k)], own_sems.at[i]
        )
        copy.start()
        own.append(copy)

    pl.semaphore_wait(barrier, devices - 1)

    def send_marks(s, d):
        pltpu.make_async_remote_copy(
            marks, all_marks.at[me], send_sems.at[0], recv_sems.at[0], (s, d), MESH
        ).start()

    to_all(send_marks)
    for j in range(1, n_sec):
        s = lax.rem(sec + j, n_sec)
        pltpu.make_async_remote_copy(
            x_src.at[s], x_all.at[sec], send_sems.at[1], recv_sems.at[1], (s, shard), MESH
        ).start()
    for i, (w, full) in enumerate(weights):
        k = w.shape[0]
        half = k // 2
        here = pl.multiple_of(core * half, half)
        there = pl.multiple_of(sec * k + core * half, half)
        for j in range(1, n_sec):
            s = lax.rem(sec + j, n_sec)
            pltpu.make_async_remote_copy(
                w.at[pl.ds(here, half)],
                full.at[pl.ds(there, half)],
                bulk_send.at[i],
                bulk_recv.at[i],
                (s, shard),
                MESH,
            ).start()

    def time_codes(b):
        for n in range(nbrs):
            x = freq[...] * gap[b, n : n + 1, :] + phase[...]
            te[b, :, n * events : (n + 1) * events] = cosine(x).astype(BF16)

    time_codes(0)

    drain(all_marks.at[pl.ds(0, devices - 1)], recv_sems.at[0])
    lane = lax.broadcasted_iota(jnp.int32, (devices, 128), 1)
    node = lax.broadcasted_iota(jnp.int32, (devices, nodes), 1)
    for b in range(BATCHES):
        row = jnp.sum(jnp.where(lane == shard, all_marks[:, b, :], 0), axis=1, keepdims=True)
        hot[b][...] = jnp.where(row == node, 1.0, 0.0).astype(BF16)
    columns = pl.ds(pl.multiple_of(sec * cols, cols), cols)
    mine = memory[:, columns]

    def send_picks(b, rows):
        for s in range(n_sec):
            block = rows[s * n_shard : (s + 1) * n_shard]
            picks_src[b][:, s, :] = block
        picks[b][shard] = picks_src[b][shard]

        def go(j, carry):
            d = lax.rem(shard + j, n_shard)
            pltpu.make_async_remote_copy(
                picks_src[b].at[d],
                picks[b].at[shard],
                send_sems.at[2 + b],
                recv_sems.at[2 + b],
                (sec, d),
                MESH,
            ).start()
            return carry

        lax.fori_loop(1, n_shard, go, 0)

    send_picks(0, dot(hot0[...], mine))
    before = dot(hot1[...], mine)
    match = dot(hot1[...], hot0[...], (1, 1))
    fresh_rows = jnp.sum(match, axis=1, keepdims=True)
    match = match.astype(BF16)

    drain(x_all.at[pl.ds(0, n_sec - 1)], recv_sems.at[1])
    for b in range(BATCHES):
        rows = jnp.concatenate(
            [x_all[s, b * pool : (b + 1) * pool, :] for s in range(n_sec)], axis=0
        )
        gates_x[b] = dot(rows.astype(BF16), w_in[...])
    time_codes(1)

    def send_parts(b):
        drain(picks[b].at[pl.ds(0, n_shard - 1)], recv_sems.at[2 + b])
        h = jnp.concatenate([picks[b][:, s, :] for s in range(n_sec)], axis=0)
        gh = dot(h.astype(BF16), w_hid[...])
        gx = gates_x[b]
        low = gx[:, : 2 * width] + gh[:, : 2 * width]
        every = jnp.concatenate([low, gx[:, 2 * width :], gh[:, 2 * width :], h, h], axis=1)
        half = every.shape[1] // 2
        for s in range(n_sec):
            block = every[s * pool : (s + 1) * pool]
            part_src[b][s] = jnp.concatenate([block[:, :half], block[:, half:]], axis=0).astype(BF16)
        part[b][sec] = part_src[b][sec]
        for j in range(1, n_sec):
            s = lax.rem(sec + j, n_sec)
            pltpu.make_async_remote_copy(
                part_src[b].at[s],
                part[b].at[sec],
                send_sems.at[4 + b],
                recv_sems.at[4 + b],
                (s, shard),
                MESH,
            ).start()

    def gru(b):
        drain(part[b].at[pl.ds(0, n_sec - 1)], recv_sems.at[4 + b])
        pieces = [part[b][s].astype(F32) for s in range(n_sec)]
        total = functools.reduce(lambda a, c: a + c, pieces)
        gates = jnp.concatenate([total[:pool], total[pool:]], axis=1)
        h = jnp.concatenate([p[pool:, -cols:] for p in pieces], axis=1)
        both = bias[0:1, :] + bias[1:2, :]
        r = jax.nn.sigmoid(gates[:, :width] + both[:, :width])
        z = jax.nn.sigmoid(gates[:, width : 2 * width] + both[:, width : 2 * width])
        gx_n = gates[:, 2 * width : 3 * width] + bias[0:1, 2 * width :]
        gh_n = gates[:, 3 * width : 4 * width] + bias[1:2, 2 * width :]
        n = jnp.tanh(gx_n + r * gh_n)
        updated = ((1.0 - z) * n + z * h).astype(BF16)
        wide = updated.astype(F32)
        for k in range(n_sec):
            back_src[b][:, k, :] = wide[:, k * cols : (k + 1) * cols]
        back[b][me] = back_src[b][shard]

        def send(s, d):
            pltpu.make_async_remote_copy(
                back_src[b].at[d],
                back[b].at[me],
                send_sems.at[6 + b],
                recv_sems.at[6 + b],
                (s, d),
                MESH,
            ).start()

        to_all(send)
        return updated

    def forward():
        for copy in own:
            copy.wait()
        for i, (w, full) in enumerate(weights):
            k = w.shape[0]
            half = k // 2
            drain(full.at[pl.ds(0, (n_sec - 1) * half)], bulk_recv.at[i])
            for j in range(1, n_sec):
                s = lax.rem(sec + j, n_sec)
                place = full.at[pl.ds(pl.multiple_of(s * k + core * half, half), half)]
                pltpu.make_async_remote_copy(
                    place, place, fwd_send.at[i], fwd_recv.at[i], (sec, sibling), MESH
                ).start()

    def gathered():
        for i, (w, full) in enumerate(weights):
            drain(full.at[pl.ds(0, (n_sec - 1) * (w.shape[0] // 2))], fwd_recv.at[i])

    def attend(b, updated):
        qkv = dot(updated, f_qkv[...])
        query = qkv[:, :width]
        keys = qkv[:, width : 2 * width].astype(BF16)
        values = qkv[:, 2 * width :].astype(BF16)
        slot = lax.broadcasted_iota(jnp.int32, (pool, events), 0)
        source = (slot == src[b : b + 1, :]).astype(F32)
        near = [(slot == nbr[b, n : n + 1, :]).astype(F32) for n in range(nbrs)]
        codes = [te[b, :, n * events : (n + 1) * events] for n in range(nbrs)]
        scale = HD ** -0.5
        mixed = []
        for head in range(HEADS):
            low = head * HD
            q_high, q_low = split(query[:, low : low + HD] * scale)
            key = keys[:, low : low + HD]
            proj = f_time[:, low : low + HD]
            pairs = dot(key, q_high, (1, 1)) + dot(key, q_low, (1, 1))
            p_high, p_low = split(pairs)
            hot_source = source.astype(BF16)
            table = dot(p_high, hot_source) + dot(p_low, hot_source)
            turned = dot(q_high, proj, (1, 1)) + dot(q_low, proj, (1, 1))
            t_high, t_low = split(turned)
            scores = []
            for n in range(nbrs):
                timed = dot(t_high, codes[n]) + dot(t_low, codes[n])
                scores.append(
                    jnp.sum(timed * source + table * near[n], axis=0, keepdims=True)
                )
            top = functools.reduce(jnp.maximum, scores)
            powers = [jnp.exp(x - top) for x in scores]
            inverse = 1.0 / functools.reduce(lambda a, c: a + c, powers)
            shares = [x * inverse for x in powers]
            by_code = shares[0] * codes[0].astype(F32)
            by_slot = shares[0] * near[0]
            for n in range(1, nbrs):
                by_code = by_code + shares[n] * codes[n].astype(F32)
                by_slot = by_slot + shares[n] * near[n]
            low_v = width + low
            mixed.append(
                dot(by_code.astype(BF16), f_time[:, low_v : low_v + HD], (0, 0))
                + dot(by_slot.astype(BF16), values[:, low : low + HD], (0, 0))
            )
        joined = jnp.concatenate(mixed, axis=1).astype(BF16)
        emb[b] = dot(joined, f_out[...]).astype(BF16)

    def returned(b, k):
        return back[b][:, k, :].astype(BF16)

    send_parts(0)
    updated0 = gru(0)
    forward()

    drain(back0.at[pl.ds(0, devices - 1)], recv_sems.at[6])
    changed = returned(0, 0)
    for k in range(1, n_sec):
        changed = jnp.where(sec == k, returned(0, k), changed)
    send_picks(1, jnp.where(fresh_rows > 0.5, dot(match, changed), before))

    def write(b, old):
        ones = jnp.ones((devices, cols), BF16)
        tile = 256
        for t in range(0, nodes, tile):
            places = hot[b][:, t : t + tile]
            hit = dot(places, ones, (0, 0)) > 0.5
            for k in range(n_sec):
                spot = slice(k * cols, (k + 1) * cols)
                new = dot(places, returned(b, k), (0, 0))
                kept = old[t : t + tile, spot].astype(F32)
                memory_out[t : t + tile, spot] = jnp.where(hit, new, kept).astype(BF16)

    write(0, memory)
    send_parts(1)
    gathered()
    attend(0, updated0)
    updated1 = gru(1)
    attend(1, updated1)
    drain(back1.at[pl.ds(0, devices - 1)], recv_sems.at[7])
    write(1, memory_out)

    drain(all_marks.at[pl.ds(0, devices - 1)], send_sems.at[0])
    drain(x_all.at[pl.ds(0, n_sec - 1)], send_sems.at[1])
    for b in range(BATCHES):
        drain(picks[b].at[pl.ds(0, n_shard - 1)], send_sems.at[2 + b])
        drain(part[b].at[pl.ds(0, n_sec - 1)], send_sems.at[4 + b])
        drain(back[b].at[pl.ds(0, devices - 1)], send_sems.at[6 + b])
    for i, (w, full) in enumerate(weights):
        rows = pl.ds(0, (n_sec - 1) * (w.shape[0] // 2))
        drain(full.at[rows], bulk_send.at[i])
        drain(full.at[rows], fwd_send.at[i])


def body(
    n_sec,
    n_shard,
    memory,
    messages,
    slot_rows,
    counts,
    src_slot,
    nbr_slots,
    time_gap,
    time_freq,
    time_phase,
    gru_input,
    gru_hidden,
    gru_bias,
    attn_qkv,
    attn_out,
    time_proj,
):
    width = memory.shape[1]
    nodes = memory.shape[0]
    pool = n_shard
    cols = width // n_sec
    events = src_slot.shape[1]
    nbrs = nbr_slots.shape[2]
    tw = time_freq.shape[0]
    devices = n_sec * n_shard
    sec = lax.axis_index("section")
    marks = jnp.where(sec < counts[:, 0, :], slot_rows[:, 0, :, 0], -1)
    marks = jnp.pad(marks, ((0, 8 - BATCHES), (0, 128 - n_shard)))
    wide = (4 * width + 2 * cols) // 2
    out = pl.pallas_call(
        functools.partial(kernel, n_sec, n_shard),
        out_shape=(
            jax.ShapeDtypeStruct((nodes, width), BF16),
            jax.ShapeDtypeStruct((BATCHES, events, width), BF16),
        ),
        in_specs=[pl.BlockSpec(memory_space=pltpu.VMEM)] * 14,
        out_specs=(pl.BlockSpec(memory_space=pltpu.VMEM),) * 2,
        scratch_shapes=[
            pltpu.VMEM((devices, 8, 128), jnp.int32),
            pltpu.VMEM((n_sec, BATCHES * pool, cols), F32),
            pltpu.VMEM((n_sec, BATCHES * pool, cols), F32),
            pltpu.VMEM((n_shard, 8, cols), F32),
            pltpu.VMEM((n_shard, 8, cols), F32),
            pltpu.VMEM((n_shard, 8, cols), F32),
            pltpu.VMEM((n_shard, 8, cols), F32),
            pltpu.VMEM((n_sec, 2 * pool, wide), BF16),
            pltpu.VMEM((n_sec, 2 * pool, wide), BF16),
            pltpu.VMEM((n_sec, 2 * pool, wide), BF16),
            pltpu.VMEM((n_sec, 2 * pool, wide), BF16),
            pltpu.VMEM((n_shard, 8, cols), F32),
            pltpu.VMEM((n_shard, 8, cols), F32),
            pltpu.VMEM((devices, 8, cols), F32),
            pltpu.VMEM((devices, 8, cols), F32),
            pltpu.VMEM((devices, nodes), BF16),
            pltpu.VMEM((devices, nodes), BF16),
            pltpu.VMEM((BATCHES, n_sec * pool, 3 * width), F32),
            pltpu.VMEM((BATCHES, tw, nbrs * events), BF16),
            pltpu.VMEM((width, 3 * width), BF16),
            pltpu.VMEM((width, width), BF16),
            pltpu.VMEM((tw, 2 * width), BF16),
            pltpu.SemaphoreType.DMA((8,)),
            pltpu.SemaphoreType.DMA((8,)),
            pltpu.SemaphoreType.DMA((3,)),
            pltpu.SemaphoreType.DMA((3,)),
            pltpu.SemaphoreType.DMA((3,)),
            pltpu.SemaphoreType.DMA((3,)),
            pltpu.SemaphoreType.DMA((3,)),
        ],
        compiler_params=pltpu.CompilerParams(
            collective_id=0, has_side_effects=True, vmem_limit_bytes=56 * 1024 * 1024
        ),
    )(
        memory,
        messages.reshape(BATCHES * pool, width),
        marks,
        src_slot,
        nbr_slots.transpose(0, 2, 1),
        time_gap.transpose(0, 2, 1),
        time_freq.reshape(tw, 1),
        time_phase.reshape(tw, 1),
        gru_input,
        gru_hidden,
        gru_bias,
        attn_qkv,
        attn_out,
        time_proj,
    )
    return out


def solution(mesh):
    in_specs = (
        P("shard", None),
        P(None, "shard", None, "section", None),
        P(None, "shard", None, "section"),
        P(None, "shard", None),
        P(None, ("section", "shard")),
        P(None, ("section", "shard"), None),
        P(None, ("section", "shard"), None),
        P(),
        P(),
        P("section", None),
        P("section", None),
        P(),
        P("section", None),
        P("section", None),
        P("section", None),
    )
    out_specs = (P("shard", None), P(None, ("section", "shard"), None))
    program = functools.partial(body, mesh.shape["section"], mesh.shape["shard"])
    return jax.shard_map(program, mesh=mesh, in_specs=in_specs, out_specs=out_specs, check_vma=False)
```

time: 217 us -> 55.5 us (0.26)
  blocking collectives: 69.6 us -> 0 us
  Pallas kernels: 0 us -> 46.1 us
  starting transfers between devices: 36.3 us -> 0 us
  matrix products: 35.1 us -> 0 us
  local copies, waits for them, and re-layouts: 37.8 us -> 8.4 us
  waiting for transfers between devices: 16.7 us -> 0 us
  between operations: 14.4 us -> 0.68 us
  other arithmetic: 6.2 us -> 0.01 us
    all_gather x8 -> x0, blocking collectives: 69.6 us -> none  [the longest x2 16.2 us: body(): lax.all_gather(got_alive, 'section', axis=1, tiled=True)]
    pallas_call x0 -> x1, Pallas kernels: none -> 46.1 us  [body(): pl.pallas_call(functools.partial(kernel, n_sec, n_shard), out_shape=(jax....]
    all_to_all x8 -> x0, starting transfers between devices: 36.2 us -> none  [the longest x2 9.87 us: body(): lax.all_to_all(alive, 'shard', split_axis=0, concat_axis=0, tiled=True)]
    dot_general x20 -> x0, matrix products: 35.1 us -> none  [the longest x2 17.1 us: embed(): jnp.einsum('ent,tc->enc', encoded, tproj, preferred_element_type=jnp.floa...]
    all_to_all x8 -> x0, waiting for transfers between devices: 15.3 us -> none  [the longest x2 11 us: body(): lax.all_to_all(alive, 'shard', split_axis=0, concat_axis=0, tiled=True)]
    gather x6 -> x0, local copies, waits for them, and re-layouts: 13 us -> none  [the longest x2 8.63 us: embed(): near = kv[nearby].astype(jnp.float32) + timed]
    convert_element_type x4 -> x0, local copies, waits for them, and re-layouts: 8.65 us -> none  [the longest x2 7.31 us: embed(): near = kv[nearby].astype(jnp.float32) + timed]
    scatter x2 -> x0, local copies, waits for them, and re-layouts: 6.18 us -> none  [body(): memory = memory.at[target].set(new_rows.reshape(-1, width), mode='drop')]
  transfers between devices with their start and end apart: 11 -> 0, of which waited for: 3 -> 0; matrix products, arithmetic and copies ran while one was open for 31% -> 0% of each run, Pallas kernels for 0% -> 0%
where the time goes in v1:
time: 55.5 us; the launch traced here: 55.2 us
  Pallas kernels  46.1 us (83%)
  local copies, waits for them, and re-layouts  8.4 us (15%)
  between operations  0.68 us (1%)
    pallas_call x1, Pallas kernels, body(): pl.pallas_call(functools.partial(kernel, n_sec, n_shard), out_shape=(jax....  46.1 us
    unnamed x18, local copies, waits for them, and re-layouts  6.31 us

profile of v1, /device:TPU:0, one launch (start us, length us, event | category | flops | bytes accessed | tf_op | source)
XLA Modules:
  0.0 55.2 jit_solution(17600132830519954197)
XLA Ops:
  0.6 0.0 copy-start.4
  0.6 0.0 copy-start.1
  0.7 0.7 %copy-done.4 = s32[2,1,8]{2,1,0:T(1,128)S(1)} copy-done((s32[2,1,8]{2,1,0:T(1,128)S(1)}, s32[2,1,8]{2,1,0:T(1,128)}, u32[]{:S(2)}) %copy-start.4) | copy-done | bytes 88
  1.3 0.0 copy-start.3
  1.3 0.7 %copy-done.3 = s32[2,1,8,1]{2,3,1,0:T(1,128)S(1)} copy-done((s32[2,1,8,1]{2,3,1,0:T(1,128)S(1)}, s32[2,1,8,1]{2,3,1,0:T(1,128)}, u32[]{:S(2)}) %copy-start.3) | copy-done | bytes 88
  2.0 0.6 %pad.4.marks = s32[8,128]{1,0:T(8,128)} pad(s32[2,8]{1,0:T(2,128)S(1)} %bitcast_select_fusion, s32[]{:T(128)} %constant.8.clone.1), padding=0_6x0_120 | pad | bytes 4164 | tf_op jit(solution)/shard_map/jit(_pad)/pad | solution.py:421
  2.6 0.0 copy-done.1
  2.6 0.0 copy-start.2
  2.6 0.6 %copy.26 = s32[2,128,10]{1,2,0:T(8,128)} copy(s32[2,128,10]{1,0,2:T(2,128)S(1)} %copy-done.1) | data formatting | bytes 20480 | tf_op args[5]
  3.2 0.1 copy-done.2
  3.3 0.6 %copy.25 = f32[2,128,10]{1,2,0:T(8,128)} copy(f32[2,128,10]{1,0,2:T(2,128)S(1)} %copy-done.2) | data formatting | bytes 20480 | tf_op args[6]
  3.9 0.0 copy-start.5
  3.9 0.7 %copy-done.5 = f32[128]{0:T(128)S(1)} copy-done((f32[128]{0:T(128)S(1)}, f32[128]{0:T(128)}, u32[]{:S(2)}) %copy-start.5) | copy-done | bytes 536
  4.6 0.0 copy-start.6
  4.6 0.7 %copy.19.freq = f32[128,1]{1,0:T(8,128)} copy(f32[128,1]{0,1:T(1,128)S(1)} %bitcast.16) | data formatting | bytes 1024 | tf_op jit(solution)/shard_map/reshape | solution.py:472
  5.3 0.0 copy-done.6
  5.3 0.7 %copy.20.phase = f32[128,1]{1,0:T(8,128)} copy(f32[128,1]{0,1:T(1,128)S(1)} %bitcast.17) | data formatting | bytes 1024 | tf_op jit(solution)/shard_map/reshape | solution.py:473
  6.1 46.1 %shard_map.158 = (bf16[1024,512]{1,0:T(8,128)(2,1)}, bf16[2,128,512]{2,1,0:T(8,128)(2,1)}) custom-call(bf16[1024,512]{1,0:T(8,128)(2,1)} %memory.1, bf16[16,512]{1,0:T(8,128)(2,1)} %bitcast.14, s32[8,128]{1,0:T(8,128)} %pad.4.marks, s32[2,128]{1,0:T(2,128)} %src.1, s32[2,10,128]{2,1,0:T(8,128)} %bitcast.12, f32[2,10,128]{2,1,0:T(8,128)} %bitcast.13, ...), custom_call_target="tpu_custom_call" | custom-call | tf_op jit(solution)/shard_map/pallas_call | solution.py:423
  52.2 0.0 copy-start
  52.2 2.3 %copy.29 = bf16[1024,512]{1,0:T(8,128)(2,1)} copy(bf16[1024,512]{1,0:T(8,128)(2,1)} %get-tuple-element.4) | data formatting | bytes 2097152
  54.5 0.0 copy-done
  54.5 0.7 %copy.30 = bf16[2,128,512]{2,1,0:T(8,128)(2,1)} copy(bf16[2,128,512]{2,1,0:T(8,128)(2,1)S(1)} %copy-done) | data formatting | bytes 524288
  (2 shorter events, 0.0 us)
Async XLA Ops:
  0.6 0.7 %copy-start.4 = (s32[2,1,8]{2,1,0:T(1,128)S(1)}, s32[2,1,8]{2,1,0:T(1,128)}, u32[]{:S(2)}) copy-start(s32[2,1,8]{2,1,0:T(1,128)} %param.18) | copy-start | bytes 196
  0.6 2.0 %copy-start.1 = (s32[2,128,10]{1,0,2:T(2,128)S(1)}, s32[2,128,10]{1,0,2:T(2,128)}, u32[]{:S(2)}) copy-start(s32[2,128,10]{1,0,2:T(2,128)} %param.20) | copy-start | bytes 30724
  1.3 0.7 %copy-start.3 = (s32[2,1,8,1]{2,3,1,0:T(1,128)S(1)}, s32[2,1,8,1]{2,3,1,0:T(1,128)}, u32[]{:S(2)}) copy-start(s32[2,1,8,1]{2,3,1,0:T(1,128)} %param.17) | copy-start | bytes 196
  2.6 0.7 %copy-start.2 = (f32[2,128,10]{1,0,2:T(2,128)S(1)}, f32[2,128,10]{1,0,2:T(2,128)}, u32[]{:S(2)}) copy-start(f32[2,128,10]{1,0,2:T(2,128)} %param.21) | copy-start | bytes 30724
  3.9 0.7 %copy-start.5 = (f32[128]{0:T(128)S(1)}, f32[128]{0:T(128)}, u32[]{:S(2)}) copy-start(f32[128]{0:T(128)} %param.22) | copy-start | bytes 1540
  4.6 0.7 %copy-start.6 = (f32[128]{0:T(128)S(1)}, f32[128]{0:T(128)}, u32[]{:S(2)}) copy-start(f32[128]{0:T(128)} %param.23) | copy-start | bytes 1540
  52.2 2.3 %copy-start = (bf16[2,128,512]{2,1,0:T(8,128)(2,1)S(1)}, bf16[2,128,512]{2,1,0:T(8,128)(2,1)}, u32[]{:S(2)}) copy-start(bf16[2,128,512]{2,1,0:T(8,128)(2,1)} %get-tuple-element.5) | copy-start | bytes 786436

commit v2 on v1

--- a/solution.py
+++ b/solution.py
@@ -36,6 +36,10 @@
     return total
 
 
+def wrap(i, n):
+    return jnp.where(i >= n, i - n, i)
+
+
 def dot(a, b, contract=(1, 0), precision=None):
     return lax.dot_general(
         a,
@@ -54,16 +58,17 @@
 def kernel(
     n_sec,
     n_shard,
-    memory,
+    memory_hbm,
     messages,
-    marks,
+    slot_rows,
+    counts,
     src,
     nbr,
     gap,
     freq,
     phase,
-    w_in,
-    w_hid,
+    w_in_hbm,
+    w_hid_hbm,
     bias,
     w_qkv,
     w_out,
@@ -99,6 +104,11 @@
     fwd_send,
     fwd_recv,
     own_sems,
+    memory,
+    w_in,
+    w_hid,
+    load_sems,
+    marks,
 ):
     sec = lax.axis_index("section")
     shard = lax.axis_index("shard")
@@ -108,8 +118,7 @@
     pool = n_shard
     cols = width // n_sec
     events = emb.shape[1]
-    nbrs = gap.shape[1]
-    tw = freq.shape[0]
+    nbrs = gap.shape[0]
     core = lax.rem(shard, 2)
     sibling = shard + 1 - 2 * core
     picks_src, picks = (picks_src0, picks_src1), (picks0, picks1)
@@ -121,13 +130,23 @@
         pltpu.make_async_copy(ref, ref, sem).wait()
 
     def to_all(step):
+        secs = [wrap(sec + j, n_sec) for j in range(n_sec)]
+
         def go(j, carry):
-            peer = lax.rem(me + j, devices)
-            step(lax.div(peer, n_shard), lax.rem(peer, n_shard))
+            d = wrap(shard + j, n_shard)
+            for s in secs:
+                step(s, d)
             return carry
 
-        lax.fori_loop(1, devices, go, 0)
-
+        for s in secs[1:]:
+            step(s, shard)
+        lax.fori_loop(1, n_shard, go, 0)
+
+    loads = []
+    for i, (far, near_ref) in enumerate(((memory_hbm, memory), (w_in_hbm, w_in), (w_hid_hbm, w_hid))):
+        load = pltpu.make_async_copy(far, near_ref, load_sems.at[i])
+        load.start()
+        loads.append(load)
     barrier = pltpu.get_barrier_semaphore()
     to_all(
         lambda s, d: pl.semaphore_signal(barrier, inc=1, device_id=(s, d), device_id_type=MESH)
@@ -136,6 +155,9 @@
     for s in range(n_sec):
         x_src[s] = messages[:, s * cols : (s + 1) * cols].astype(F32)
     x_all[sec] = x_src[sec]
+    marks[...] = jnp.full(marks.shape, -1, jnp.int32)
+    for b in range(BATCHES):
+        marks[b : b + 1, 0:n_shard] = jnp.where(sec < counts[b], slot_rows[b], -1)
     all_marks[me] = marks[...]
     weights = ((w_qkv, f_qkv), (w_out, f_out), (w_time, f_time))
     own = []
@@ -156,7 +178,7 @@
 
     to_all(send_marks)
     for j in range(1, n_sec):
-        s = lax.rem(sec + j, n_sec)
+        s = wrap(sec + j, n_sec)
         pltpu.make_async_remote_copy(
             x_src.at[s], x_all.at[sec], send_sems.at[1], recv_sems.at[1], (s, shard), MESH
         ).start()
@@ -166,7 +188,7 @@
         here = pl.multiple_of(core * half, half)
         there = pl.multiple_of(sec * k + core * half, half)
         for j in range(1, n_sec):
-            s = lax.rem(sec + j, n_sec)
+            s = wrap(sec + j, n_sec)
             pltpu.make_async_remote_copy(
                 w.at[pl.ds(here, half)],
                 full.at[pl.ds(there, half)],
@@ -176,9 +198,12 @@
                 MESH,
             ).start()
 
+    freq_column = jnp.transpose(jnp.broadcast_to(freq[...], (8, freq.shape[1])))[:, :1]
+    phase_column = jnp.transpose(jnp.broadcast_to(phase[...], (8, phase.shape[1])))[:, :1]
+
     def time_codes(b):
         for n in range(nbrs):
-            x = freq[...] * gap[b, n : n + 1, :] + phase[...]
+            x = freq_column * gap[n, b : b + 1, :] + phase_column
             te[b, :, n * events : (n + 1) * events] = cosine(x).astype(BF16)
 
     time_codes(0)
@@ -190,6 +215,7 @@
         row = jnp.sum(jnp.where(lane == shard, all_marks[:, b, :], 0), axis=1, keepdims=True)
         hot[b][...] = jnp.where(row == node, 1.0, 0.0).astype(BF16)
     columns = pl.ds(pl.multiple_of(sec * cols, cols), cols)
+    loads[0].wait()
     mine = memory[:, columns]
 
     def send_picks(b, rows):
@@ -199,7 +225,7 @@
         picks[b][shard] = picks_src[b][shard]
 
         def go(j, carry):
-            d = lax.rem(shard + j, n_shard)
+            d = wrap(shard + j, n_shard)
             pltpu.make_async_remote_copy(
                 picks_src[b].at[d],
                 picks[b].at[shard],
@@ -218,6 +244,7 @@
     fresh_rows = jnp.sum(match, axis=1, keepdims=True)
     match = match.astype(BF16)
 
+    loads[1].wait()
     drain(x_all.at[pl.ds(0, n_sec - 1)], recv_sems.at[1])
     for b in range(BATCHES):
         rows = jnp.concatenate(
@@ -225,6 +252,7 @@
         )
         gates_x[b] = dot(rows.astype(BF16), w_in[...])
     time_codes(1)
+    loads[2].wait()
 
     def send_parts(b):
         drain(picks[b].at[pl.ds(0, n_shard - 1)], recv_sems.at[2 + b])
@@ -239,7 +267,7 @@
             part_src[b][s] = jnp.concatenate([block[:, :half], block[:, half:]], axis=0).astype(BF16)
         part[b][sec] = part_src[b][sec]
         for j in range(1, n_sec):
-            s = lax.rem(sec + j, n_sec)
+            s = wrap(sec + j, n_sec)
             pltpu.make_async_remote_copy(
                 part_src[b].at[s],
                 part[b].at[sec],
@@ -288,7 +316,7 @@
             half = k // 2
             drain(full.at[pl.ds(0, (n_sec - 1) * half)], bulk_recv.at[i])
             for j in range(1, n_sec):
-                s = lax.rem(sec + j, n_sec)
+                s = wrap(sec + j, n_sec)
                 place = full.at[pl.ds(pl.multiple_of(s * k + core * half, half), half)]
                 pltpu.make_async_remote_copy(
                     place, place, fwd_send.at[i], fwd_recv.at[i], (sec, sibling), MESH
@@ -305,26 +333,30 @@
         values = qkv[:, 2 * width :].astype(BF16)
         slot = lax.broadcasted_iota(jnp.int32, (pool, events), 0)
         source = (slot == src[b : b + 1, :]).astype(F32)
-        near = [(slot == nbr[b, n : n + 1, :]).astype(F32) for n in range(nbrs)]
+        hot_source = source.astype(BF16)
+        near = [(slot == nbr[n, b : b + 1, :]).astype(F32) for n in range(nbrs)]
         codes = [te[b, :, n * events : (n + 1) * events] for n in range(nbrs)]
         scale = HD ** -0.5
-        mixed = []
+        mixed, turned, tables = [], [], []
         for head in range(HEADS):
             low = head * HD
-            q_high, q_low = split(query[:, low : low + HD] * scale)
-            key = keys[:, low : low + HD]
+            q = jnp.concatenate(split(query[:, low : low + HD] * scale), axis=0)
             proj = f_time[:, low : low + HD]
-            pairs = dot(key, q_high, (1, 1)) + dot(key, q_low, (1, 1))
-            p_high, p_low = split(pairs)
-            hot_source = source.astype(BF16)
-            table = dot(p_high, hot_source) + dot(p_low, hot_source)
-            turned = dot(q_high, proj, (1, 1)) + dot(q_low, proj, (1, 1))
-            t_high, t_low = split(turned)
+            pairs = dot(keys[:, low : low + HD], q, (1, 1))
+            p_high, p_low = split(pairs[:, :pool] + pairs[:, pool:])
+            tables.append(dot(p_high, hot_source) + dot(p_low, hot_source))
+            both = dot(q, proj, (1, 1))
+            turned.append(both[:pool] + both[pool:])
+        turned = jnp.concatenate(turned, axis=0)
+        timed = dot(jnp.concatenate(split(turned), axis=0), te[b])
+        timed = timed[: HEADS * pool] + timed[HEADS * pool :]
+        for head in range(HEADS):
+            low = head * HD
             scores = []
             for n in range(nbrs):
-                timed = dot(t_high, codes[n]) + dot(t_low, codes[n])
+                here = timed[head * pool : (head + 1) * pool, n * events : (n + 1) * events]
                 scores.append(
-                    jnp.sum(timed * source + table * near[n], axis=0, keepdims=True)
+                    jnp.sum(here * source + tables[head] * near[n], axis=0, keepdims=True)
                 )
             top = functools.reduce(jnp.maximum, scores)
             powers = [jnp.exp(x - top) for x in scores]
@@ -348,7 +380,6 @@
 
     send_parts(0)
     updated0 = gru(0)
-    forward()
 
     drain(back0.at[pl.ds(0, devices - 1)], recv_sems.at[6])
     changed = returned(0, 0)
@@ -357,18 +388,21 @@
     send_picks(1, jnp.where(fresh_rows > 0.5, dot(match, changed), before))
 
     def write(b, old):
-        ones = jnp.ones((devices, cols), BF16)
+        rows = [returned(b, k) for k in range(n_sec)]
+        rows = jnp.concatenate(rows + [jnp.ones((devices, cols), BF16)], axis=1)
         tile = 256
         for t in range(0, nodes, tile):
-            places = hot[b][:, t : t + tile]
-            hit = dot(places, ones, (0, 0)) > 0.5
+            new = dot(hot[b][:, t : t + tile], rows, (0, 0))
+            hit = new[:, width:] > 0.5
             for k in range(n_sec):
                 spot = slice(k * cols, (k + 1) * cols)
-                new = dot(places, returned(b, k), (0, 0))
-                kept = old[t : t + tile, spot].astype(F32)
-                memory_out[t : t + tile, spot] = jnp.where(hit, new, kept).astype(BF16)
+                kept = old[t : t + tile, spot]
+                memory_out[t : t + tile, spot] = jnp.where(
+                    hit, new[:, spot], kept.astype(F32)
+                ).astype(BF16)
 
     write(0, memory)
+    forward()
     send_parts(1)
     gathered()
     attend(0, updated0)
@@ -416,9 +450,8 @@
     nbrs = nbr_slots.shape[2]
     tw = time_freq.shape[0]
     devices = n_sec * n_shard
-    sec = lax.axis_index("section")
-    marks = jnp.where(sec < counts[:, 0, :], slot_rows[:, 0, :, 0], -1)
-    marks = jnp.pad(marks, ((0, 8 - BATCHES), (0, 128 - n_shard)))
+    far = pl.BlockSpec(memory_space=pl.ANY)
+    near = pl.BlockSpec(memory_space=pltpu.VMEM)
     wide = (4 * width + 2 * cols) // 2
     out = pl.pallas_call(
         functools.partial(kernel, n_sec, n_shard),
@@ -426,7 +459,7 @@
             jax.ShapeDtypeStruct((nodes, width), BF16),
             jax.ShapeDtypeStruct((BATCHES, events, width), BF16),
         ),
-        in_specs=[pl.BlockSpec(memory_space=pltpu.VMEM)] * 14,
+        in_specs=[far] + [near] * 8 + [far] * 2 + [near] + [far] * 3,
         out_specs=(pl.BlockSpec(memory_space=pltpu.VMEM),) * 2,
         scratch_shapes=[
             pltpu.VMEM((devices, 8, 128), jnp.int32),
@@ -458,6 +491,11 @@
             pltpu.SemaphoreType.DMA((3,)),
             pltpu.SemaphoreType.DMA((3,)),
             pltpu.SemaphoreType.DMA((3,)),
+            pltpu.VMEM((nodes, width), BF16),
+            pltpu.VMEM(gru_input.shape, BF16),
+            pltpu.VMEM(gru_hidden.shape, BF16),
+            pltpu.SemaphoreType.DMA((3,)),
+            pltpu.VMEM((8, 128), jnp.int32),
         ],
         compiler_params=pltpu.CompilerParams(
             collective_id=0, has_side_effects=True, vmem_limit_bytes=56 * 1024 * 1024
@@ -465,12 +503,13 @@
     )(
         memory,
         messages.reshape(BATCHES * pool, width),
-        marks,
+        slot_rows.reshape(BATCHES, 1, n_shard),
+        counts,
         src_slot,
-        nbr_slots.transpose(0, 2, 1),
-        time_gap.transpose(0, 2, 1),
-        time_freq.reshape(tw, 1),
-        time_phase.reshape(tw, 1),
+        nbr_slots.transpose(2, 0, 1),
+        time_gap.transpose(2, 0, 1),
+        time_freq.reshape(1, tw),
+        time_phase.reshape(1, tw),
         gru_input,
         gru_hidden,
         gru_bias,

time: 55.5 us -> 49.3 us (0.89)
  local copies, waits for them, and re-layouts: 8.4 us -> 3.01 us
  Pallas kernels: 46.1 us -> 45.5 us
    unnamed x18 -> x4, local copies, waits for them, and re-layouts: 6.31 us -> 3.01 us
    reshape x2 -> x0, local copies, waits for them, and re-layouts: 1.48 us -> none  [the longest x1 0.74 us: body(): time_phase.reshape(tw, 1)]
    pallas_call x1, Pallas kernels: 46.1 us -> 45.5 us  [body(): pl.pallas_call(functools.partial(kernel, n_sec, n_shard), out_shape=(jax....]
    pad x1 -> x0, local copies, waits for them, and re-layouts: 0.6 us -> none  [body(): marks = jnp.pad(marks, ((0, 8 - BATCHES), (0, 128 - n_shard)))]
where the time goes in v2:
time: 49.3 us; the launch traced here: 49.1 us
  Pallas kernels  45.5 us (92%)
  local copies, waits for them, and re-layouts  3.01 us (6%)
  between operations  0.65 us (1%)
    pallas_call x1, Pallas kernels, body(): pl.pallas_call(functools.partial(kernel, n_sec, n_shard), out_shape=(jax....  45.5 us
    unnamed x4, local copies, waits for them, and re-layouts  3.01 us

profile of v2, /device:TPU:0, one launch (start us, length us, event | category | flops | bytes accessed | tf_op | source)
XLA Modules:
  0.0 49.1 jit_solution(17815060320515198668)
XLA Ops:
  0.6 45.5 %shard_map.158 = (bf16[1024,512]{1,0:T(8,128)(2,1)}, bf16[2,128,512]{2,1,0:T(8,128)(2,1)}) custom-call(bf16[1024,512]{1,0:T(8,128)(2,1)} %memory_hbm.1, bf16[16,512]{1,0:T(8,128)(2,1)} %bitcast.8, s32[2,1,8]{2,1,0:T(1,128)} %bitcast.11, s32[2,1,8]{2,1,0:T(1,128)} %counts.1, s32[2,128]{1,0:T(2,128)} %src.1, s32[10,2,128]{2,1,0:T(2,128)} %bitcast.9, ...), custom_call_target="tpu_custom_call" | custom-call | tf_op jit(solution)/shard_map/pallas_call | solution.py:456
  46.1 0.0 copy-start
  46.1 2.3 %copy.20 = bf16[1024,512]{1,0:T(8,128)(2,1)} copy(bf16[1024,512]{1,0:T(8,128)(2,1)} %get-tuple-element.4) | data formatting | bytes 2097152
  48.4 0.0 copy-done
  48.4 0.7 %copy.21 = bf16[2,128,512]{2,1,0:T(8,128)(2,1)} copy(bf16[2,128,512]{2,1,0:T(8,128)(2,1)S(1)} %copy-done) | data formatting | bytes 524288
Async XLA Ops:
  46.1 2.3 %copy-start = (bf16[2,128,512]{2,1,0:T(8,128)(2,1)S(1)}, bf16[2,128,512]{2,1,0:T(8,128)(2,1)}, u32[]{:S(2)}) copy-start(bf16[2,128,512]{2,1,0:T(8,128)(2,1)} %get-tuple-element.5) | copy-start | bytes 786436
